TPU v7x, 256 devices: a whole 4x4x8 slice. The times are simulated.
256 devices in a mesh: tok: 64 (over z, y, core), feat: 4 (over x).
Axes of the slice: x: 4, y: 4, z: 8, core: 2. Of those that a mesh axis runs over, the one named last changes fastest.
Arguments:
- doc_in: bfloat16 [512, 8192], P(None, 'tok'), may hold values from -6 to 6
- query_in: bfloat16 [256, 8192], P(None, 'tok'), may hold values from -6 to 6
- doc_grad: bfloat16 [512, 28672], P('tok', 'feat'), may hold values from -6 to 6
- query_grad: bfloat16 [256, 28672], P('tok', 'feat'), may hold values from -6 to 6
- doc_ids: int32 [512], replicated, may hold values from 0 to 3, as said below
- query_ids: int32 [256], replicated, may hold values from 0 to 1, as said below
- in_basis: bfloat16 [8192, 8192], P('tok', 'feat'), may hold values from -0.0625 to 0.0625
- out_basis: bfloat16 [28672, 28672], P('feat', 'tok'), may hold values from -0.03125 to 0.03125
- eigvals: float32 [8192, 28672], P('feat', 'tok'), may hold values from 0.1 to 10
Outputs:
- ihvp: bfloat16 [8192, 28672], P('feat', 'tok')
- scores: float32 [2, 4], replicated
Inputs may be any that keep to these rules, and one draw needn't show every extreme that they name: `doc_ids`: never falling along the tokens; every document has 1 to 256 tokens, one exactly that many. `query_ids`: one transcript has exactly 192 tokens, the other the remaining 256 // 4; their tokens may lie anywhere.
All inputs are finite; a program needn't handle non-finite values.
Results may differ from a plain program's by a relative error of at most 0.012.
Values may be sent and summed in bfloat16 or wider, within the bound.
A program may use at most 128 MiB of HBM per device.

v0:
```python
import math

import jax
import jax.numpy as jnp
from jax import lax
from jax.sharding import PartitionSpec as P

D_IN = 8192
D_OUT = 28672
DOCS = 4
QUERIES = 2
DOC_TOK = 512
QUERY_TOK = 256


damping = 0.1


def shards(
    doc_in, query_in, doc_grad, query_grad, doc_ids, query_ids, in_basis, out_basis, eigvals
):
    members = lax.axis_size("tok")
    doc_local = doc_grad.shape[0]
    local_grad = jnp.concatenate([doc_grad, query_grad], 0)
    gathered = lax.all_gather(local_grad, "tok", axis=0, tiled=True)
    partial_value = jnp.dot(gathered, out_basis, preferred_element_type=jnp.float32)
    width = partial_value.shape[1]
    partial_value = partial_value.reshape(members, -1, width)
    doc_part = partial_value[:, :doc_local].reshape(-1, width)
    query_part = partial_value[:, doc_local:].reshape(-1, width)
    doc_sum, query_sum = lax.psum((doc_part, query_part), "feat")
    doc_out_rot = doc_sum.astype(jnp.bfloat16)
    query_out_rot = query_sum.astype(jnp.bfloat16)
    doc_in_part = jnp.dot(doc_in, in_basis, preferred_element_type=jnp.float32)
    query_in_part = jnp.dot(query_in, in_basis, preferred_element_type=jnp.float32)
    doc_sum_in, query_sum_in = lax.psum((doc_in_part, query_in_part), "tok")
    doc_in_rot = doc_sum_in.astype(jnp.bfloat16)
    query_in_rot = query_sum_in.astype(jnp.bfloat16)
    doc_hot = (doc_ids[:, None] == jnp.arange(DOCS, dtype=jnp.int32)[None, :]).astype(jnp.float32)
    query_hot = (query_ids[:, None] == jnp.arange(QUERIES, dtype=jnp.int32)[None, :]).astype(
        jnp.bfloat16
    )
    damped = (eigvals + damping) * (1.0 / math.sqrt(QUERY_TOK))
    precs = []
    for query in range(QUERIES):
        masked = query_in_rot * query_hot[:, query : query + 1]
        grad_q = lax.dot_general(
            masked, query_out_rot, (((0,), (0,)), ((), ())), preferred_element_type=jnp.float32
        )
        precs.append((grad_q / damped).astype(jnp.bfloat16))
    total = precs[0].astype(jnp.float32)
    query = 1
    total = total + precs[query].astype(jnp.float32)
    ihvp = total.astype(jnp.bfloat16)
    projected = jnp.dot(doc_in_rot, jnp.concatenate(precs, 1), preferred_element_type=jnp.float32)
    doc_out_f = doc_out_rot.astype(jnp.float32)
    token_rows = []
    for query in range(QUERIES):
        token_rows.append(
            jnp.sum(projected[:, query * width : (query + 1) * width] * doc_out_f, axis=1)
        )
    token_score = jnp.stack(token_rows, 0)
    local_scores = jnp.dot(token_score, doc_hot, precision=lax.Precision.HIGHEST)
    scores = lax.psum(local_scores, ("tok", "feat")) / math.sqrt(D_IN * D_OUT * DOC_TOK)
    return (ihvp, scores)


def solution(mesh):
    placed = (
        P(None, "tok"),
        P(None, "tok"),
        P("tok", "feat"),
        P("tok", "feat"),
        P(),
        P(),
        P("tok", "feat"),
        P("feat", "tok"),
        P("feat", "tok"),
    )
    return jax.shard_map(
        shards, mesh=mesh, in_specs=placed, out_specs=(P("feat", "tok"), P()), check_vma=False
    )
```

profile of v0, /device:TPU:1, one launch (start us, length us, event | category | flops | bytes accessed | tf_op | source)
XLA Modules:
  0.0 478.4 jit_solution(14929257529651589133)
XLA Ops:
  7.2 0.0 copy-start
  7.2 0.0 copy-start.1
  7.2 0.0 all-gather.3.cloned.1.call-start
  7.2 1.7 maximum_bitcast_fusion
  8.9 0.0 all-gather.3.cloned.1.call-update
  9.0 0.0 copy-done
  9.0 0.0 copy-start.2
  9.0 3.6 fusion.24
  12.6 0.0 copy-done.1
  12.6 0.4 fusion.22
  13.0 0.0 copy-done.2
  13.0 305.1 %all-reduce.5 = (bf16[256,2048]{1,0:T(8,128)(2,1)}, bf16[512,2048]{1,0:T(8,128)(2,1)}) all-reduce(f32[256,2048]{1,0:T(8,128)S(1)} %fusion.22, f32[512,2048]{1,0:T(8,128)} %fusion.24), channel_id=1, replica_groups=mesh['tok'=64,'feat'=4] {'tok'}, use_global_device_ids=true, to_apply=%region_0.0 | all-reduce | flops 1572864 | bytes 9437184 | tf_op jit(solution)/shard_map/psum | solution.py:36
  318.1 15.9 %reshape.19 = bf16[768,7168]{1,0:T(8,128)(2,1)} reshape(bf16[64,12,7168]{2,1,0:T(8,128)(2,1)} %all-gather.3.cloned.1.call-done) | data formatting | bytes 22020096
  334.0 11.4 %fusion.23 = f32[768,448]{1,0:T(8,128)} fusion(bf16[768,7168]{1,0:T(8,128)(2,1)} %reshape.19, bf16[7168,448]{0,1:T(8,128)(2,1)} %param.16), kind=kOutput, calls=%fused_computation.36 | convolution fusion | flops 4932501504 | bytes 18808832 | tf_op jit(solution)/shard_map/dot_general | solution.py:26
  345.4 1.5 reshape.15
  346.9 1.1 slice_bitcast_fusion
  348.0 0.1 slice.25
  348.1 0.2 reshape.16
  348.2 32.6 %all-reduce.4 = (bf16[256,448]{1,0:T(8,128)(2,1)S(1)}, bf16[512,448]{1,0:T(8,128)(2,1)S(1)}) all-reduce(f32[256,448]{1,0:T(8,128)S(1)} %reshape.16, f32[512,448]{1,0:T(8,128)} %slice_bitcast_fusion), channel_id=1, replica_groups=mesh['tok'=64,'feat'=4] {'feat'}, use_global_device_ids=true, to_apply=%region_1.0 | all-reduce | flops 344064 | bytes 2064384 | tf_op jit(solution)/shard_map/psum | solution.py:31
  380.8 0.0 copy-start.3
  380.8 0.0 copy-start.5
  380.8 3.3 divide_convert_fusion.1
  384.1 0.1 copy-done.3
  384.3 0.3 copy-done.5
  384.6 2.4 add_convert_fusion
  387.0 0.0 copy-done.4
  387.0 2.4 fusion
  389.3 0.7 fusion.5
  390.0 0.0 copy-done.6
  390.0 0.3 fusion.13
  390.3 80.7 %psum.39 = f32[2,4]{1,0:T(2,128)S(1)} all-reduce(f32[2,4]{1,0:T(2,128)S(1)} %fusion.13), channel_id=1, replica_groups=mesh['tok'=64,'feat'=4] {'tok','feat'}, use_global_device_ids=true, to_apply=%region_6.0 | all-reduce | flops 8 | bytes 64 | tf_op jit(solution)/shard_map/psum | solution.py:64
  470.9 0.6 broadcast_multiply_fusion
  (5 shorter events, 0.0 us)
Async XLA Ops:
  7.2 1.8 copy-start
  7.2 5.4 %copy-start.1 = (bf16[256,128]{1,0:T(8,128)(2,1)S(1)}, bf16[256,128]{1,0:T(8,128)(2,1)}, u32[]{:S(2)}) copy-start(bf16[256,128]{1,0:T(8,128)(2,1)} %param.10) | copy-start | bytes 196612
  7.2 310.9 %all-gather.3.cloned.1.call-start = ((), (), s32[]{:S(2)}) async-start(), calls=%async_computation | async-start | bytes 14909440 | tf_op jit(solution)/shard_map/all_gather | solution.py:25
  9.0 4.0 copy-start.2
  380.8 3.5 copy-start.3
  380.8 3.7 copy-start.5
  384.6 2.4 copy-start.4
  387.0 3.0 copy-start.6
Sparse Core Ops, SparseCore 0:
  11.3 106.5 all-gather.2
where the time goes:
time: 479 us; the launch traced here: 478 us
  blocking collectives  418 us (87%)
  matrix products  23.7 us (5%)
  local copies, waits for them, and re-layouts  19.2 us (4%)
  between operations  14.2 us (3%)
    psum x1, blocking collectives, shards(): doc_sum_in, query_sum_in = lax.psum((doc_in_part, query_in_part), 'tok')  305 us
    psum x1, blocking collectives, shards(): lax.psum(local_scores, ('tok', 'feat')) / math.sqrt(D_IN * D_OUT * DOC_TOK)  80.7 us
    psum x1, blocking collectives, shards(): doc_sum, query_sum = lax.psum((doc_part, query_part), 'feat')  32.6 us
    unnamed x15, local copies, waits for them, and re-layouts  16.4 us
    dot_general x1, matrix products, shards(): jnp.dot(gathered, out_basis, preferred_element_type=jnp.float32)  11.4 us
  transfers between devices with their start and end apart: 1, of which 0 were waited for; matrix products, arithmetic and copies ran while one was open for 1% of the time, Pallas kernels for 0%

commit v1 on v0

v1 whole, which is shorter than its diff:
```python
import functools
import math

import jax
import jax.numpy as jnp
from jax import lax
from jax.experimental import pallas as pl
from jax.experimental.pallas import tpu as pltpu
from jax.sharding import PartitionSpec as P

DOCS = 4
QUERIES = 2
DAMPING = 0.1
Y = 4
CORES = 2
RS_DT = jnp.float32
X_DT = jnp.float32
F32 = jnp.float32
BF16 = jnp.bfloat16
MESH = pl.DeviceIdType.MESH
N_SEM = 400


def ds(i, size):
    return pl.ds(pl.multiple_of(i * size, size), size)


def kernel(
    Z, X, scale,
    doc_in, query_in, doc_grad, query_grad, doc_ids, query_ids, in_basis, out_basis, eigvals,
    ihvp, scores,
    inq, ind, inb, gd_own, gd_oth, gq_own, gq_oth, gq_f, gd, gq, gq2, bown, both, eig,
    pin_q, pin_d, zs_q, zr_q, zs_d, zr_d, zsum_q, zsum_d, ys_q, yr_q, ys_d, yr_d, rot_q, rot_d,
    p_own, p_oth, p_rcv, x_snd, x_rcv, out_rot, mq, prec, ih, proj, sc_a, sc_b, sc_c,
    ssem, rsem, lsem,
):
    tok, x = lax.axis_index("tok"), lax.axis_index("feat")
    c = lax.rem(tok, CORES)
    y = lax.rem(lax.div(tok, CORES), Y)
    z = lax.div(tok, CORES * Y)
    oc = 1 - c

    def dev(zz, yy, cc, xx):
        return ((zz * Y + yy) * CORES + cc, xx)

    def wrap(v, n):
        return lax.rem(v + 4 * n, n)

    partner = dev(z, y, oc, x)

    def to_z(step):
        return dev(wrap(z + step, Z), y, c, x)

    def to_y(step):
        return dev(z, wrap(y + step, Y), c, x)

    G = CORES * X
    m = c * X + x

    def to_m(step):
        mm = wrap(m + step, G)
        return dev(z, y, lax.div(mm, X), lax.rem(mm, X))

    barrier = pltpu.get_barrier_semaphore()
    friends = [to_m(k) for k in range(1, G)] + [to_y(k) for k in range(1, Y)] + [to_z(k) for k in range(1, Z)]
    for friend in friends:
        pl.semaphore_signal(barrier, inc=1, device_id=friend, device_id_type=MESH)

    locals_ = []

    def local(src, dst):
        copy = pltpu.make_async_copy(src, dst, lsem.at[len(locals_)])
        copy.start()
        locals_.append(copy)
        return copy

    F = doc_grad.shape[1]
    half = F // 2
    quarter = half // 2
    wc = in_basis.shape[1] // CORES
    nf = in_basis.shape[0]

    l_gq = local(query_grad.at[:, ds(c, half)], gq_own)
    l_inq = local(query_in, inq.at[:, ds(c, nf)])
    l_inb = local(in_basis.at[:, ds(c, wc)], inb.at[ds(c, nf), :])
    l_ind = local(doc_in, ind.at[:, ds(c, nf)])
    l_gd = local(doc_grad.at[:, ds(c, half)], gd_own)
    l_b = local(out_basis.at[ds(c, half), :], bown)
    l_eig = local(eigvals, eig)

    pl.semaphore_wait(barrier, len(friends))

    sent = []

    def send(src, dst, to):
        i = len(sent)
        copy = pltpu.make_async_remote_copy(
            src_ref=src, dst_ref=dst, send_sem=ssem.at[i], recv_sem=rsem.at[i], device_id=to, device_id_type=MESH
        )
        copy.start()
        sent.append(copy)
        return copy

    r_gq = send(query_grad.at[:, ds(oc, half)], gq_oth, partner)
    r_inq = send(query_in, inq.at[:, ds(c, nf)], partner)
    r_inb = send(in_basis.at[:, ds(oc, wc)], inb.at[ds(c, nf), :], partner)
    r_ind = send(doc_in, ind.at[:, ds(c, nf)], partner)
    r_gd = send(doc_grad.at[:, ds(oc, half)], gd_oth, partner)
    r_b = send(out_basis.at[ds(oc, half), :], both, partner)

    def ring_ag(p, n, blk, half_of, to, arrived=lambda k: None):
        h = n // 2
        r = send(blk(p), blk(p), to(1))
        l = send(blk(p), blk(p), to(-1))
        for s in range(1, h):
            yield
            k = wrap(p - s, n)
            r.wait_recv()
            if s < h - 1:
                r = send(blk(k), blk(k), to(1))
            else:
                r = send(half_of(k, 0), half_of(k, 0), to(1))
            arrived(k)
            k = wrap(p + s, n)
            l.wait_recv()
            if s < h - 1:
                l = send(blk(k), blk(k), to(-1))
            else:
                l = send(half_of(k, 1), half_of(k, 1), to(-1))
            arrived(k)
        yield
        r.wait_recv()
        l.wait_recv()
        arrived(wrap(p + h, n))

    def ring_rs(p, n, part, snd, rcv, width, to, done):
        h = n // 2
        lo, hi = slice(0, width // 2), slice(width // 2, width)
        r_half, l_half = rcv.at[0, 0, :, lo], rcv.at[1, 0, :, hi]
        snd[0, 0] = part(wrap(p + h, n)).astype(snd.dtype)
        r = send(snd.at[0, 0, :, lo], r_half, to(1))
        l = send(snd.at[0, 0, :, hi], l_half, to(-1))
        for s in range(1, h):
            yield
            own = part(wrap(p + h - s, n))
            r.wait_recv()
            if s == 1:
                snd[0, s, :, lo] = (own[:, lo] + rcv[0, 0, :, lo].astype(F32)).astype(snd.dtype)
                snd[0, s, :, hi] = own[:, hi].astype(snd.dtype)
            else:
                snd[0, s] = (own + rcv[0, s - 1].astype(F32)).astype(snd.dtype)
            r = send(snd.at[0, s], rcv.at[0, s], to(1))
            own = part(wrap(p - h + s, n))
            l.wait_recv()
            if s == 1:
                snd[1, s, :, lo] = own[:, lo].astype(snd.dtype)
                snd[1, s, :, hi] = (own[:, hi] + rcv[1, 0, :, hi].astype(F32)).astype(snd.dtype)
            else:
                snd[1, s] = (own + rcv[1, s - 1].astype(F32)).astype(snd.dtype)
            l = send(snd.at[1, s], rcv.at[1, s], to(-1))
        yield
        own = part(p)
        r.wait_recv()
        l.wait_recv()
        done(own + rcv[0, h - 1].astype(F32) + rcv[1, h - 1].astype(F32))

    def gd_blk(zz, yy):
        return gd.at[ds(zz * Y + yy, 2 * doc_grad.shape[0]), :]

    def gd_half(zz, yy, k):
        return gd.at[ds(zz * Y + yy, 2 * doc_grad.shape[0]), pl.ds(k * (half // 2), half // 2)]

    def gq_blk(zz, yy):
        return gq.at[zz * Y + yy]

    def gq_half(zz, yy, k):
        return gq.at[zz * Y + yy, :, pl.ds(k * (quarter // 2), quarter // 2)]

    y_q, y_d = [], []

    def spawn_q(zz):
        y_q.append(ring_ag(y, Y, lambda k: gq_blk(zz, k), lambda k, b: gq_half(zz, k, b), to_y))

    def spawn_d(zz):
        y_d.append(ring_ag(y, Y, lambda k: gd_blk(zz, k), lambda k, b: gd_half(zz, k, b), to_y))

    live = []

    def y_step(window=4):
        while len(live) < window and (y_q or y_d):
            task = (y_q or y_d).pop(0)
            next(task)
            live.append(task)
        if not live:
            return False
        task = live.pop(0)
        if next(task, "end") != "end":
            live.append(task)
        return True

    nq = query_grad.shape[0]
    first = c == 0
    l_gq.wait()
    r_gq.wait_recv()
    own, oth = gq_own[...].astype(F32), gq_oth[...].astype(F32)
    gq_f[0:nq, :] = jnp.where(first, own, oth)
    gq_f[nq : 2 * nq, :] = jnp.where(first, oth, own)
    me_zy = z * Y + y
    gq[me_zy] = jnp.concatenate([gq_f[:, 0:quarter], gq_f[:, quarter:half]], axis=0).astype(BF16)
    ag_q = ring_ag(z, Z, lambda k: gq_blk(k, y), lambda k, b: gq_half(k, y, b), to_z, spawn_q)
    next(ag_q)
    spawn_q(z)
    y_step_start = y_q.pop(0)
    next(y_step_start)
    live.append(y_step_start)

    dq, dd = query_in.shape[0], doc_in.shape[0]
    bq, bd = dq // Z, dd // Z
    wy = wc // Y
    for copy in (l_inq, l_inb):
        copy.wait()
    for copy in (r_inq, r_inb):
        copy.wait_recv()
    pin_q[...] = jnp.dot(inq[...], inb[...], preferred_element_type=F32)

    def put_zq(v):
        zsum_q[...] = v

    def put_zd(v):
        zsum_d[...] = v

    rs_q = ring_rs(z, Z, lambda k: pin_q[ds(k, bq), :], zs_q, zr_q, wc, to_z, put_zq)
    next(rs_q)
    l_ind.wait()
    r_ind.wait_recv()

    pin_d[...] = jnp.dot(ind[...], inb[...], preferred_element_type=F32)
    rs_d = ring_rs(z, Z, lambda k: pin_d[ds(k, bd), :], zs_d, zr_d, wc, to_z, put_zd)
    next(rs_d)

    l_gd.wait()
    r_gd.wait_recv()
    own, oth = gd_own[...].astype(F32), gd_oth[...].astype(F32)
    gd[ds(me_zy, 2 * doc_grad.shape[0]), :] = jnp.concatenate(
        [jnp.where(first, own, oth), jnp.where(first, oth, own)], axis=0
    ).astype(BF16)
    ag_d = ring_ag(z, Z, lambda k: gd_blk(k, y), lambda k, b: gd_half(k, y, b), to_z, spawn_d)
    next(ag_d)
    spawn_d(z)

    for _ in range(Z // 2):
        next(rs_q, None)
        next(rs_d, None)
        next(ag_q, None)
        next(ag_d, None)
        for _ in range(4):
            y_step()

    def rows_of(rot, b, k, col, width):
        return rot.at[ds(k, b), ds(col, width)]

    def in_task(rot, zsum, ys, yr, b):
        def part(k):
            return zsum[:, ds(k, wy)]

        def put(v):
            rot[ds(z, b), ds(c * Y + y, wy)] = v.astype(BF16)

        yield from ring_rs(y, Y, part, ys, yr, wy, to_y, put)
        yield from ring_ag(
            y, Y, lambda k: rows_of(rot, b, z, c * Y + k, wy),
            lambda k, h: rows_of(rot, b, z, (c * Y + k) * 2 + h, wy // 2), to_y,
        )
        yield from ring_ag(
            z, Z, lambda k: rows_of(rot, b, k, c, wc),
            lambda k, h: rows_of(rot, b, k, c * 2 + h, wc // 2), to_z,
        )
        whole = rot.at[:, ds(c, wc)]
        copy = send(whole, whole, partner)
        yield
        copy.wait_recv()

    in_q = in_task(rot_q, zsum_q, ys_q, yr_q, bq)
    in_d = in_task(rot_d, zsum_d, ys_d, yr_d, bd)
    next(in_q)
    next(in_d)

    def matmul(lhs, b, out, row, rows, tile=896):
        depth = lhs.shape[1]
        tile = math.gcd(depth, tile)
        out[row : row + rows, :] = jnp.dot(
            lhs[:, 0:tile], b[0:tile, :], preferred_element_type=F32
        )

        def body(k, _):
            out[row : row + rows, :] += jnp.dot(lhs[:, ds(k, tile)], b[ds(k, tile), :], preferred_element_type=F32)
            return 0

        lax.fori_loop(1, depth // tile, body, 0)

    def out_task(lhs, row, rows):
        span = slice(row, row + rows)
        share = rows // X
        base = row // X
        matmul(lhs, both, p_oth, row, rows)
        swap = send(p_oth.at[span, :], p_rcv.at[span, :], partner)
        matmul(lhs, bown, p_own, row, rows)
        yield
        swap.wait_recv()
        total = p_own[span, :] + p_rcv[span, :]
        p_own[span, :] = total
        x_snd[span, :] = total.astype(X_DT)
        copies = []
        for k in range(1, X):
            to = wrap(x + k, X)
            copies.append(
                send(
                    x_snd.at[pl.ds(pl.multiple_of(row + to * share, share), share), :],
                    x_rcv.at[x, pl.ds(base, share), :],
                    dev(z, y, c, to),
                )
            )
        yield
        for copy in copies:
            copy.wait_recv()
        mine = pl.ds(pl.multiple_of(row + x * share, share), share)
        x_rcv[x, pl.ds(base, share), :] = x_snd[mine, :]
        total = x_rcv[0, pl.ds(base, share), :].astype(F32)
        for k in range(1, X):
            total = total + x_rcv[k, pl.ds(base, share), :].astype(F32)
        out_rot[mine, :] = total.astype(BF16)
        copies = []
        for k in range(1, X):
            copies.append(send(out_rot.at[mine, :], out_rot.at[mine, :], dev(z, y, c, wrap(x + k, X))))
        yield
        for copy in copies:
            copy.wait_recv()

    for _ in range(5 + Z // 2 - 2):
        next(in_q, None)
        next(in_d, None)
        for _ in range(2):
            y_step()

    while y_step():
        pass
    l_b.wait()
    r_b.wait_recv()

    for h in range(2):
        rows = gq.shape[1] // 2
        gq2[:, h * quarter : (h + 1) * quarter] = (
            gq[:, h * rows : (h + 1) * rows, :].astype(F32).reshape(dq, quarter).astype(BF16)
        )
    out_q = out_task(gq2, 0, dq)
    next(out_q)
    next(in_q, None)
    next(in_d, None)
    next(out_q)
    out_d = out_task(gd, dq, dd)
    next(out_d)
    next(out_q)
    next(out_d)
    next(out_q, None)

    ids_q = jnp.broadcast_to(query_ids[...].astype(F32), (128, dq)).T[:, 0:1]
    for q in range(QUERIES):
        mq[q] = jnp.where(ids_q == float(q), out_rot[0:dq, :].astype(F32), 0.0).astype(BF16)
    l_eig.wait()
    for _ in range(2):
        next(in_q, None)

    tile = 256
    n_tiles = eig.shape[0] // tile

    def ih_copy(i):
        return pltpu.make_async_copy(ih.at[ds(i, tile), :], ihvp.at[ds(i, tile), :], lsem.at[16 + i])

    def precondition(i, _):
        at = ds(i, tile)
        factor = math.sqrt(dq) / (eig[at, :] + DAMPING)
        lhs = rot_q[:, at]
        total = None
        for q in range(QUERIES):
            grad = lax.dot_general(lhs, mq[q], (((0,), (0,)), ((), ())), preferred_element_type=F32)
            block = (grad * factor).astype(BF16)
            prec[q, at, :] = block
            block = block.astype(F32)
            total = block if total is None else total + block
        ih[at, :] = total.astype(BF16)
        ih_copy(i).start()
        return 0

    lax.fori_loop(0, n_tiles, precondition, 0)
    next(out_d)
    for _ in range(2):
        next(in_d, None)

    for q in range(QUERIES):
        matmul(rot_d, prec.at[q], proj.at[q], 0, dd, 512)
    next(out_d, None)

    ids_d = jnp.broadcast_to(doc_ids[...].astype(F32), (128, dd)).T
    lane = lax.broadcasted_iota(jnp.int32, (dd, 128), 1).astype(F32)
    hot = (ids_d == lane).astype(F32)
    row_id = lax.broadcasted_iota(jnp.int32, (8, 128), 0)
    value = jnp.zeros((8, 128), F32)
    for q in range(QUERIES):
        token = jnp.sum(proj[q] * out_rot[dq : dq + dd, :].astype(F32), axis=1, keepdims=True)
        per_doc = jnp.sum(token * hot, axis=0, keepdims=True)
        value = jnp.where(row_id == q, per_doc, value)

    def exchange(buf, me, n, to, value):
        buf[me] = value
        copies = [send(buf.at[me], buf.at[me], to(k)) for k in range(1, n)]
        for copy in copies:
            copy.wait_recv()
        return jnp.sum(buf[...], axis=0)

    value = exchange(sc_a, m, G, to_m, value)
    value = exchange(sc_b, y, Y, to_y, value)
    value = exchange(sc_c, z, Z, to_z, value)
    scores[...] = value[0:QUERIES, 0:DOCS] * scale

    def ih_wait(i, _):
        ih_copy(i).wait()
        return 0

    lax.fori_loop(0, n_tiles, ih_wait, 0)
    for copy in sent:
        copy.wait_send()


def shards(
    Z, X, doc_in, query_in, doc_grad, query_grad, doc_ids, query_ids, in_basis, out_basis, eigvals
):
    dd, dq = doc_in.shape[0], query_in.shape[0]
    F, cols = out_basis.shape
    half, quarter = F // 2, F // 4
    nf, width = in_basis.shape
    wc = width // CORES
    wy = wc // Y
    bq, bd = dq // Z, dd // Z
    hz, hy = Z // 2, Y // 2
    n_docs, n_q = doc_grad.shape[0], query_grad.shape[0]
    scale = 1.0 / math.sqrt(width * X * cols * Z * Y * CORES * dd)
    vmem = pltpu.VMEM
    any_ = pl.BlockSpec(memory_space=pl.ANY)
    in_vmem = pl.BlockSpec(memory_space=pltpu.VMEM)
    return pl.pallas_call(
        functools.partial(kernel, Z, X, scale),
        out_shape=(
            jax.ShapeDtypeStruct((width, cols), BF16),
            jax.ShapeDtypeStruct((QUERIES, DOCS), F32),
        ),
        in_specs=[any_, any_, any_, any_, in_vmem, in_vmem, any_, any_, any_],
        out_specs=(any_, in_vmem),
        scratch_shapes=[
            vmem((dq, CORES * nf), BF16), vmem((dd, CORES * nf), BF16), vmem((CORES * nf, wc), BF16),
            vmem((n_docs, half), BF16), vmem((n_docs, half), BF16),
            vmem((n_q, half), BF16), vmem((n_q, half), BF16), vmem((2 * n_q, half), F32),
            vmem((dd, half), BF16), vmem((Z * Y, 4 * n_q, quarter), BF16), vmem((dq, half), BF16),
            vmem((half, cols), BF16), vmem((half, cols), BF16), vmem((width, cols), F32),
            vmem((dq, wc), F32), vmem((dd, wc), F32),
            vmem((2, hz, bq, wc), RS_DT), vmem((2, hz, bq, wc), RS_DT),
            vmem((2, hz, bd, wc), RS_DT), vmem((2, hz, bd, wc), RS_DT),
            vmem((bq, wc), F32), vmem((bd, wc), F32),
            vmem((2, hy, bq, wy), F32), vmem((2, hy, bq, wy), F32),
            vmem((2, hy, bd, wy), F32), vmem((2, hy, bd, wy), F32),
            vmem((dq, width), BF16), vmem((dd, width), BF16),
            vmem((dq + dd, cols), F32), vmem((dq + dd, cols), F32), vmem((dq + dd, cols), F32),
            vmem((dq + dd, cols), X_DT), vmem((X, (dq + dd) // X, cols), X_DT), vmem((dq + dd, cols), BF16),
            vmem((QUERIES, dq, cols), BF16), vmem((QUERIES, width, cols), BF16), vmem((width, cols), BF16),
            vmem((QUERIES, dd, cols), F32),
            vmem((CORES * X, 8, 128), F32), vmem((Y, 8, 128), F32), vmem((Z, 8, 128), F32),
            pltpu.SemaphoreType.DMA((N_SEM,)), pltpu.SemaphoreType.DMA((N_SEM,)), pltpu.SemaphoreType.DMA((32,)),
        ],
        compiler_params=pltpu.CompilerParams(
            collective_id=0, has_side_effects=True, vmem_limit_bytes=62 * 1024 * 1024
        ),
    )(
        doc_in, query_in, doc_grad, query_grad, doc_ids.reshape(1, dd), query_ids.reshape(1, dq),
        in_basis, out_basis, eigvals,
    )


def solution(mesh):
    placed = (
        P(None, "tok"),
        P(None, "tok"),
        P("tok", "feat"),
        P("tok", "feat"),
        P(),
        P(),
        P("tok", "feat"),
        P("feat", "tok"),
        P("feat", "tok"),
    )
    X = mesh.shape["feat"]
    Z = mesh.shape["tok"] // (Y * CORES)
    return jax.shard_map(
        functools.partial(shards, Z, X), mesh=mesh, in_specs=placed, out_specs=(P("feat", "tok"), P()), check_vma=False
    )
```

time: 479 us -> 169 us (0.35)
  blocking collectives: 418 us -> 0 us
  Pallas kernels: 0 us -> 148 us
  matrix products: 23.7 us -> 0 us
  between operations: 14.2 us -> 0.64 us
    psum x3 -> x0, blocking collectives: 418 us -> none  [the longest x1 305 us: shards(): doc_sum_in, query_sum_in = lax.psum((doc_in_part, query_in_part), 'tok')]
    pallas_call x0 -> x1, Pallas kernels: none -> 148 us  [shards(): pl.pallas_call(functools.partial(kernel, Z, X, scale), out_shape=(jax.Sha...]
    dot_general x7 -> x0, matrix products: 23.7 us -> none  [the longest x1 11.4 us: shards(): jnp.dot(gathered, out_basis, preferred_element_type=jnp.float32)]
    unnamed x15 -> x3, local copies, waits for them, and re-layouts: 16.4 us -> 16.3 us
  transfers between devices with their start and end apart: 1 -> 0, of which waited for: 0 -> 0; matrix products, arithmetic and copies ran while one was open for 1% -> 0% of each run, Pallas kernels for 0% -> 0%
where the time goes in v1:
time: 169 us; the launch traced here: 168 us
  Pallas kernels  148 us (88%)
  local copies, waits for them, and re-layouts  20.1 us (12%)
    pallas_call x1, Pallas kernels, shards(): pl.pallas_call(functools.partial(kernel, Z, X, scale), out_shape=(jax.Sha...  148 us
    unnamed x3, local copies, waits for them, and re-layouts  16.3 us
    pallas_call x1, local copies, waits for them, and re-layouts, shards(): pl.pallas_call(functools.partial(kernel, Z, X, scale), out_shape=(jax.Sha...  3.86 us

profile of v1, /device:TPU:1, one launch (start us, length us, event | category | flops | bytes accessed | tf_op | source)
XLA Modules:
  0.0 168.3 jit_solution(2781054977600952699)
XLA Ops:
  0.6 5.1 %copy.12.eigvals = f32[2048,448]{1,0:T(8,128)} copy(f32[2048,448]{0,1:T(8,128)} %param.17) | data formatting | bytes 7340032 | tf_op args[8]
  5.8 9.9 %copy.11.out_basis = bf16[7168,448]{1,0:T(8,128)(2,1)} copy(bf16[7168,448]{0,1:T(8,128)(2,1)} %param.16) | data formatting | bytes 12845056 | tf_op args[7]
  15.7 147.5 %shard_map.104 = (bf16[2048,448]{1,0:T(8,128)(2,1)}, f32[2,4]{1,0:T(2,128)}) custom-call(bf16[512,128]{1,0:T(8,128)(2,1)} %doc_in.1, bf16[256,128]{1,0:T(8,128)(2,1)} %query_in.1, bf16[8,7168]{1,0:T(8,128)(2,1)} %doc_grad.1, bf16[4,7168]{1,0:T(4,128)(2,1)} %query_grad.1, s32[1,512]{1,0:T(1,128)} %bitcast.2, s32[1,256]{1,0:T(1,128)} %bitcast.3, ...), custom_call_target="tpu_custom_call" | custom-call | tf_op jit(solution)/shard_map/pallas_call | solution.py:450
  163.2 3.9 %copy.13 = bf16[2048,448]{0,1:T(8,128)(2,1)} copy(bf16[2048,448]{1,0:T(8,128)(2,1)} %get-tuple-element.2) | data formatting | bytes 3670016 | tf_op jit(solution)/shard_map/pallas_call | solution.py:450
  167.1 1.2 copy.15

commit v2 on v1

v2 whole, which is shorter than its diff:
```python
import functools
import math

import jax
import jax.numpy as jnp
from jax import lax
from jax.experimental import pallas as pl
from jax.experimental.pallas import tpu as pltpu
from jax.sharding import PartitionSpec as P

DOCS = 4
QUERIES = 2
DAMPING = 0.1
Y = 4
CORES = 2
RS_DT = jnp.bfloat16
X_DT = jnp.float32
F32 = jnp.float32
BF16 = jnp.bfloat16
MESH = pl.DeviceIdType.MESH
N_SEM = 256
PLAN = (
    "yd0", "q", "yq1", "yq7", "Q", "yq0", "q", "yq2", "D", "Q", "q", "yd0", "yq1", "yq7", "yq0", "yq6", "yq2", "Q",
    "q", "yd0", "yq3", "yq1", "yq5", "D", "yq7", "yq4", "Q", "d", "yq6", "yq2", "yq3", "yq5", "yq4", "Q", "D",
    "yq6", "yq3", "d", "yd1", "yd7", "yq5", "Q", "yq4", "oq", "yd1", "D", "Q", "yd7", "d", "yd2", "yd6", "oq",
    "yd1", "o0", "Q", "D", "yd7", "Q", "o0", "d", "yd3", "yd5", "yd2", "Q", "oq", "Q", "yd6", "d", "yd4", "D", "o0",
    "yd3", "oq", "P", "yd5", "yd2", "o0", "D", "yd6", "o3", "yd4", "yd3", "o1", "o3", "yd5", "D", "yd4", "o2", "o1",
    "o2", "o3", "D", "o1", "D", "o2", "o3", "D", "R", "o1", "o2",
)


def ds(i, size):
    return pl.ds(pl.multiple_of(i * size, size), size)


def kernel(
    Z, X, scale,
    doc_in, query_in, doc_grad, query_grad, doc_ids, query_ids, in_basis, out_basis, eigvals,
    ihvp, scores,
    inq, ind, inb, gd_own, gd_oth, gq_own, gq_oth, gq_f, gd, gq, gq2, bb, eig,
    pin_q, pin_d, zs_q, zr_q, zs_d, zr_d, yr_q, yr_d, rot_q, rot_d,
    part, p_rcv, x_snd, x_rcv, out_rot, mq, prec, ih, proj, sc_a, sc_b, sc_c,
    ssem, rsem, lsem,
):
    tok, x = lax.axis_index("tok"), lax.axis_index("feat")
    c = lax.rem(tok, CORES)
    y = lax.rem(lax.div(tok, CORES), Y)
    z = lax.div(tok, CORES * Y)
    oc = 1 - c

    def dev(zz, yy, cc, xx):
        return ((zz * Y + yy) * CORES + cc, xx)

    def wrap(v, n):
        return lax.rem(v + 4 * n, n)

    partner = dev(z, y, oc, x)

    def to_z(step):
        return dev(wrap(z + step, Z), y, c, x)

    def to_y(step):
        return dev(z, wrap(y + step, Y), c, x)

    G = CORES * X
    m = c * X + x

    def to_m(step):
        mm = wrap(m + step, G)
        return dev(z, y, lax.div(mm, X), lax.rem(mm, X))

    barrier = pltpu.get_barrier_semaphore()
    friends = [to_m(k) for k in range(1, G)] + [to_y(k) for k in range(1, Y)] + [to_z(k) for k in range(1, Z)]
    for friend in friends:
        pl.semaphore_signal(barrier, inc=1, device_id=friend, device_id_type=MESH)

    locals_ = []

    def local(src, dst):
        copy = pltpu.make_async_copy(src, dst, lsem.at[len(locals_)])
        copy.start()
        locals_.append(copy)
        return copy

    F = doc_grad.shape[1]
    half = F // 2
    quarter = half // 2
    wc = in_basis.shape[1] // CORES
    nf = in_basis.shape[0]

    l_gq = local(query_grad.at[:, ds(c, half)], gq_own)
    l_inq = local(query_in, inq.at[:, ds(c, nf)])
    l_inb = local(in_basis.at[:, ds(c, wc)], inb.at[ds(c, nf), :])
    l_ind = local(doc_in, ind.at[:, ds(c, nf)])
    l_gd = local(doc_grad.at[:, ds(c, half)], gd_own)
    cols = out_basis.shape[0]
    theirs, ours = bb.at[0:cols, :], bb.at[cols : 2 * cols, :]
    l_b = local(out_basis.at[:, ds(c, half)], ours)
    l_eig = local(eigvals, eig)

    pl.semaphore_wait(barrier, len(friends))

    sent = []

    def send(src, dst, to):
        i = len(sent)
        copy = pltpu.make_async_remote_copy(
            src_ref=src, dst_ref=dst, send_sem=ssem.at[i], recv_sem=rsem.at[i], device_id=to, device_id_type=MESH
        )
        copy.start()
        sent.append(copy)
        return copy

    r_gq = send(query_grad.at[:, ds(oc, half)], gq_oth, partner)
    r_inq = send(query_in, inq.at[:, ds(c, nf)], partner)
    r_inb = send(in_basis.at[:, ds(oc, wc)], inb.at[ds(c, nf), :], partner)
    r_ind = send(doc_in, ind.at[:, ds(c, nf)], partner)
    r_gd = send(doc_grad.at[:, ds(oc, half)], gd_oth, partner)
    r_b = send(out_basis.at[:, ds(oc, half)], theirs, partner)

    def ring_ag(n, blk, there, to):
        h = n // 2

        def forward(o, step, b):
            return send(blk(o, b), there(o, step, b), to(step))

        r, l = forward(0, 1, None), forward(0, -1, None)
        for s in range(1, h):
            yield
            r.wait_recv()
            r = forward(-s, 1, None if s < h - 1 else 0)
            l.wait_recv()
            l = forward(s, -1, None if s < h - 1 else 1)
        yield
        r.wait_recv()
        l.wait_recv()

    def ring_rs(p, n, own_part, snd, rcv, width, to, done):
        h = n // 2
        lo, hi = slice(0, width // 2), slice(width // 2, width)
        r_half, l_half = rcv.at[0, 0, :, lo], rcv.at[1, 0, :, hi]
        snd[0, 0] = own_part(wrap(p + h, n)).astype(snd.dtype)
        r = send(snd.at[0, 0, :, lo], r_half, to(1))
        l = send(snd.at[0, 0, :, hi], l_half, to(-1))
        for s in range(1, h):
            yield
            own = own_part(wrap(p + h - s, n))
            r.wait_recv()
            if s == 1:
                snd[0, s, :, lo] = (own[:, lo] + rcv[0, 0, :, lo].astype(F32)).astype(snd.dtype)
                snd[0, s, :, hi] = own[:, hi].astype(snd.dtype)
            else:
                snd[0, s] = (own + rcv[0, s - 1].astype(F32)).astype(snd.dtype)
            r = send(snd.at[0, s], rcv.at[0, s], to(1))
            own = own_part(wrap(p - h + s, n))
            l.wait_recv()
            if s == 1:
                snd[1, s, :, lo] = own[:, lo].astype(snd.dtype)
                snd[1, s, :, hi] = (own[:, hi] + rcv[1, 0, :, hi].astype(F32)).astype(snd.dtype)
            else:
                snd[1, s] = (own + rcv[1, s - 1].astype(F32)).astype(snd.dtype)
            l = send(snd.at[1, s], rcv.at[1, s], to(-1))
        yield
        own = own_part(p)
        r.wait_recv()
        l.wait_recv()
        done(own + rcv[0, h - 1].astype(F32) + rcv[1, h - 1].astype(F32))

    rows_d = 2 * doc_grad.shape[0]

    def gd_blk(oz, yy, b=None):
        at = pl.ds(pl.multiple_of((oz % Z) * Y * rows_d + yy * rows_d, rows_d), rows_d)
        return gd.at[at, :] if b is None else gd.at[at, pl.ds(b * quarter, quarter)]

    def gq_blk(oz, yy, b=None):
        at = wrap(z + oz, Z) * Y + yy
        return gq.at[at] if b is None else gq.at[at, :, pl.ds(b * (quarter // 2), quarter // 2)]

    def along_y(blk, oz):
        def place(o, b):
            return blk(oz, wrap(y + o, Y), b)

        return ring_ag(Y, place, lambda o, step, b: place(o, b), to_y)

    tasks = {}
    for oz in range(Z):
        tasks["yq%d" % oz] = along_y(gq_blk, oz)
        tasks["yd%d" % oz] = along_y(gd_blk, oz)

    nq = query_grad.shape[0]
    first = c == 0
    l_gq.wait()
    r_gq.wait_recv()
    own, oth = gq_own[...].astype(F32), gq_oth[...].astype(F32)
    gq_f[0:nq, :] = jnp.where(first, own, oth)
    gq_f[nq : 2 * nq, :] = jnp.where(first, oth, own)
    gq[z * Y + y] = jnp.concatenate([gq_f[:, 0:quarter], gq_f[:, quarter:half]], axis=0).astype(BF16)
    ag_q = ring_ag(Z, lambda o, b: gq_blk(o, y, b), lambda o, step, b: gq_blk(o, y, b), to_z)
    tasks["q"] = ag_q
    next(ag_q)
    next(tasks["yq0"])

    dq, dd = query_in.shape[0], doc_in.shape[0]
    bq, bd = dq // Z, dd // Z
    wy = wc // Y
    for copy in (l_inq, l_inb):
        copy.wait()
    for copy in (r_inq, r_inb):
        copy.wait_recv()
    pin_q[...] = jnp.dot(inq[...], inb[...], preferred_element_type=F32)

    def in_task(pin, zs, zr, yr, rot, rows, place):
        def put(v):
            for k in range(Y):
                yr[Y + k] = v[:, k * wy : (k + 1) * wy]

        yield from ring_rs(z, Z, lambda k: pin[ds(k, rows), :], zs, zr, wc, to_z, put)
        copies = [send(yr.at[Y + wrap(y + k, Y)], yr.at[y], to_y(k)) for k in range(1, Y)]
        yr[y] = yr[Y + y]
        yield
        for copy in copies:
            copy.wait_recv()
        total = yr[0]
        for k in range(1, Y):
            total = total + yr[k]
        mine = rot.at[place(0), ds(c * Y + y, wy)]
        mine[...] = total.astype(BF16)
        copies = [send(mine, mine, to_y(k)) for k in range(1, Y)]
        yield
        for copy in copies:
            copy.wait_recv()

        def at(o, b):
            return rot.at[place(o), ds(c, wc) if b is None else ds(c * 2 + b, wc // 2)]

        def there(o, step, b):
            return rot.at[place(o, step), ds(c, wc) if b is None else ds(c * 2 + b, wc // 2)]

        yield from ring_ag(Z, at, there, to_z)
        whole = rot.at[:, ds(c, wc)]
        copy = send(whole, whole, partner)
        yield
        copy.wait_recv()

    in_q = in_task(pin_q, zs_q, zr_q, yr_q, rot_q, bq, lambda o, step=0: ds(wrap(z + o, Z), bq))
    in_d = in_task(
        pin_d, zs_d, zr_d, yr_d, rot_d, bd, lambda o, step=0: pl.ds(((o - step) % Z) * bd, bd)
    )
    next(in_q)
    l_ind.wait()
    r_ind.wait_recv()
    pin_d[...] = jnp.dot(ind[...], inb[...], preferred_element_type=F32)
    next(in_d)

    l_gd.wait()
    r_gd.wait_recv()
    own, oth = gd_own[...].astype(F32), gd_oth[...].astype(F32)
    gd[ds(y, rows_d), :] = jnp.concatenate(
        [jnp.where(first, own, oth), jnp.where(first, oth, own)], axis=0
    ).astype(BF16)
    ag_d = ring_ag(Z, lambda o, b: gd_blk(o, y, b), lambda o, step, b: gd_blk(o - step, y, b), to_z)
    tasks.update(d=ag_d, Q=in_q, D=in_d)

    def matmul(a, b, out, at, tile):
        depth = a.shape[1]
        tile = math.gcd(depth, tile)
        contract = (((1,), (1,)), ((), ()))
        out[:, at] = lax.dot_general(a[:, 0:tile], b[:, 0:tile], contract, preferred_element_type=F32)

        def body(k, _):
            out[:, at] += lax.dot_general(a[:, ds(k, tile)], b[:, ds(k, tile)], contract, preferred_element_type=F32)
            return 0

        lax.fori_loop(1, depth // tile, body, 0)

    share = cols // X

    def out_task(grads, at):
        matmul(bb, grads, part, at, 896)
        swap = send(part.at[0:cols, at], p_rcv.at[:, at], partner)
        yield
        swap.wait_recv()
        x_snd[:, at] = (part[cols : 2 * cols, at] + p_rcv[:, at]).astype(X_DT)
        copies = []
        for k in range(1, X):
            to = wrap(x + k, X)
            copies.append(send(x_snd.at[ds(to, share), at], x_rcv.at[x, :, at], dev(z, y, c, to)))
        yield
        for copy in copies:
            copy.wait_recv()
        mine = ds(x, share)
        x_rcv[x, :, at] = x_snd[mine, at]
        total = x_rcv[0, :, at].astype(F32)
        for k in range(1, X):
            total = total + x_rcv[k, :, at].astype(F32)
        out_rot[mine, at] = total.astype(BF16)
        copies = []
        for k in range(1, X):
            copies.append(send(out_rot.at[mine, at], out_rot.at[mine, at], dev(z, y, c, wrap(x + k, X))))
        yield
        for copy in copies:
            copy.wait_recv()

    def out_queries():
        l_b.wait()
        r_b.wait_recv()
        rows = gq.shape[1] // 2
        for h in range(2):
            gq2[:, h * quarter : (h + 1) * quarter] = (
                gq[:, h * rows : (h + 1) * rows, :].astype(F32).reshape(dq, quarter).astype(BF16)
            )
        yield from out_task(gq2, slice(0, dq))

    chunk = 2 * (dd // Z)
    tasks["oq"] = out_queries()
    for i in range(Z // 2):
        tasks["o%d" % i] = out_task(
            gd.at[i * chunk : (i + 1) * chunk, :], slice(dq + i * chunk, dq + (i + 1) * chunk)
        )

    tile = 256
    n_tiles = eig.shape[1] // tile

    def ih_copy(i):
        return pltpu.make_async_copy(ih.at[:, ds(i, tile)], ihvp.at[:, ds(i, tile)], lsem.at[16 + i])

    def precondition(i, _):
        at = ds(i, tile)
        factor = math.sqrt(dq) / (eig[:, at] + DAMPING)
        grad = jnp.dot(mq[...], rot_q[:, at], preferred_element_type=F32)
        total = None
        for q in range(QUERIES):
            block = (grad[q * cols : (q + 1) * cols] * factor).astype(BF16)
            prec[q * cols : (q + 1) * cols, at] = block
            block = block.astype(F32)
            total = block if total is None else total + block
        ih[:, at] = total.astype(BF16)
        ih_copy(i).start()
        return 0

    def precondition_all():
        ids_q = query_ids[...]
        for q in range(QUERIES):
            mq[q * cols : (q + 1) * cols, :] = jnp.where(ids_q == q, out_rot[:, 0:dq].astype(F32), 0.0).astype(BF16)
        l_eig.wait()
        lax.fori_loop(0, n_tiles, precondition, 0)
        yield

    def project():
        matmul(prec, rot_d, proj, slice(0, dd), 512)
        yield

    tasks.update(P=precondition_all(), R=project())
    for name in PLAN:
        next(tasks[name], None)
    for task in tasks.values():
        for _ in task:
            pass

    ids_d = pltpu.roll(jnp.broadcast_to(doc_ids[...], (8, dd)), dd - z * (dd // Z), 1)
    hot = ids_d == lax.broadcasted_iota(jnp.int32, (8, dd), 0)
    row_id = lax.broadcasted_iota(jnp.int32, (8, 128), 0)
    lane_id = lax.broadcasted_iota(jnp.int32, (8, 128), 1)
    value = jnp.zeros((8, 128), F32)
    for q in range(QUERIES):
        token = jnp.sum(
            proj[q * cols : (q + 1) * cols, :] * out_rot[:, dq : dq + dd].astype(F32), axis=0, keepdims=True
        )
        per_doc = jnp.sum(jnp.where(hot, token, 0.0), axis=1, keepdims=True)
        for d in range(DOCS):
            value = jnp.where((row_id == q) & (lane_id == d), per_doc[d : d + 1, :], value)

    def exchange(buf, me, n, to, value):
        buf[me] = value
        copies = [send(buf.at[me], buf.at[me], to(k)) for k in range(1, n)]
        for copy in copies:
            copy.wait_recv()
        return jnp.sum(buf[...], axis=0)

    value = exchange(sc_a, m, G, to_m, value)
    value = exchange(sc_b, y, Y, to_y, value)
    value = exchange(sc_c, z, Z, to_z, value)
    scores[...] = value[0:QUERIES, 0:DOCS] * scale

    def ih_wait(i, _):
        ih_copy(i).wait()
        return 0

    lax.fori_loop(0, n_tiles, ih_wait, 0)
    for copy in sent:
        copy.wait_send()


def shards(
    Z, X, doc_in, query_in, doc_grad, query_grad, doc_ids, query_ids, in_basis, out_basis, eigvals
):
    dd, dq = doc_in.shape[0], query_in.shape[0]
    out_basis = out_basis.T
    cols, F = out_basis.shape
    half, quarter = F // 2, F // 4
    nf, width = in_basis.shape
    wc = width // CORES
    wy = wc // Y
    bq, bd = dq // Z, dd // Z
    hz = Z // 2
    n_docs, n_q = doc_grad.shape[0], query_grad.shape[0]
    scale = 1.0 / math.sqrt(width * X * cols * Z * Y * CORES * dd)
    vmem = pltpu.VMEM
    any_ = pl.BlockSpec(memory_space=pl.ANY)
    in_vmem = pl.BlockSpec(memory_space=pltpu.VMEM)
    ihvp, scores = pl.pallas_call(
        functools.partial(kernel, Z, X, scale),
        out_shape=(
            jax.ShapeDtypeStruct((cols, width), BF16),
            jax.ShapeDtypeStruct((QUERIES, DOCS), F32),
        ),
        in_specs=[any_, any_, any_, any_, in_vmem, in_vmem, any_, any_, any_],
        out_specs=(any_, in_vmem),
        scratch_shapes=[
            vmem((dq, CORES * nf), BF16), vmem((dd, CORES * nf), BF16), vmem((CORES * nf, wc), BF16),
            vmem((n_docs, half), BF16), vmem((n_docs, half), BF16),
            vmem((n_q, half), BF16), vmem((n_q, half), BF16), vmem((2 * n_q, half), F32),
            vmem((dd, half), BF16), vmem((Z * Y, 4 * n_q, quarter), BF16), vmem((dq, half), BF16),
            vmem((2 * cols, half), BF16), vmem((cols, width), F32),
            vmem((dq, wc), F32), vmem((dd, wc), F32),
            vmem((2, hz, bq, wc), RS_DT), vmem((2, hz, bq, wc), RS_DT),
            vmem((2, hz, bd, wc), RS_DT), vmem((2, hz, bd, wc), RS_DT),
            vmem((2 * Y, bq, wy), F32), vmem((2 * Y, bd, wy), F32),
            vmem((dq, width), BF16), vmem((dd, width), BF16),
            vmem((2 * cols, dq + dd), F32), vmem((cols, dq + dd), F32),
            vmem((cols, dq + dd), X_DT), vmem((X, cols // X, dq + dd), X_DT), vmem((cols, dq + dd), BF16),
            vmem((QUERIES * cols, dq), BF16), vmem((QUERIES * cols, width), BF16), vmem((cols, width), BF16),
            vmem((QUERIES * cols, dd), F32),
            vmem((CORES * X, 8, 128), F32), vmem((Y, 8, 128), F32), vmem((Z, 8, 128), F32),
            pltpu.SemaphoreType.DMA((N_SEM,)), pltpu.SemaphoreType.DMA((N_SEM,)), pltpu.SemaphoreType.DMA((32,)),
        ],
        compiler_params=pltpu.CompilerParams(
            collective_id=0, has_side_effects=True, vmem_limit_bytes=62 * 1024 * 1024
        ),
    )(
        doc_in, query_in, doc_grad, query_grad, doc_ids.reshape(1, dd), query_ids.reshape(1, dq),
        in_basis, out_basis, eigvals.T,
    )
    return ihvp.T, scores


def solution(mesh):
    placed = (
        P(None, "tok"),
        P(None, "tok"),
        P("tok", "feat"),
        P("tok", "feat"),
        P(),
        P(),
        P("tok", "feat"),
        P("feat", "tok"),
        P("feat", "tok"),
    )
    X = mesh.shape["feat"]
    Z = mesh.shape["tok"] // (Y * CORES)
    return jax.shard_map(
        functools.partial(shards, Z, X), mesh=mesh, in_specs=placed, out_specs=(P("feat", "tok"), P()), check_vma=False
    )
```

time: 169 us -> 105 us (0.62)
  Pallas kernels: 148 us -> 101 us
  local copies, waits for them, and re-layouts: 20.1 us -> 3.51 us
    pallas_call x1, Pallas kernels: 148 us -> 101 us  [shards(): pl.pallas_call(functools.partial(kernel, Z, X, scale), out_shape=(jax.Sha...]
    unnamed x3 -> x4, local copies, waits for them, and re-layouts: 16.3 us -> 3.51 us
    pallas_call x1 -> x0, local copies, waits for them, and re-layouts: 3.86 us -> none  [shards(): pl.pallas_call(functools.partial(kernel, Z, X, scale), out_shape=(jax.Sha...]
where the time goes in v2:
time: 105 us
  Pallas kernels  101 us (96%)
  local copies, waits for them, and re-layouts  3.51 us (3%)
    pallas_call x1, Pallas kernels, shards(): pl.pallas_call(functools.partial(kernel, Z, X, scale), out_shape=(jax.Sha...  101 us
    unnamed x4, local copies, waits for them, and re-layouts  3.51 us

profile of v2, /device:TPU:1, one launch (start us, length us, event | category | flops | bytes accessed | tf_op | source)
XLA Modules:
  0.0 104.7 jit_solution(8841057016806726153)
XLA Ops:
  0.6 100.6 %shard_map.104 = (bf16[448,2048]{1,0:T(8,128)(2,1)}, f32[2,4]{1,0:T(2,128)}) custom-call(bf16[512,128]{1,0:T(8,128)(2,1)} %doc_in.1, bf16[256,128]{1,0:T(8,128)(2,1)} %query_in.1, bf16[8,7168]{1,0:T(8,128)(2,1)} %doc_grad.1, bf16[4,7168]{1,0:T(4,128)(2,1)} %query_grad.1, s32[1,512]{1,0:T(1,128)} %bitcast.8, s32[1,256]{1,0:T(1,128)} %bitcast.9, ...), custom_call_target="tpu_custom_call" | custom-call | tf_op jit(solution)/shard_map/pallas_call | solution.py:411
  101.2 0.0 copy-start
  101.2 2.9 %copy.13 = bf16[2048,448]{0,1:T(8,128)(2,1)} copy(bf16[2048,448]{0,1:T(8,128)(2,1)} %bitcast.7) | data formatting | bytes 3670016
  104.2 0.0 copy-done
  104.2 0.6 copy.14
Async XLA Ops:
  101.2 3.0 %copy-start = (f32[2,4]{1,0:T(2,128)S(1)}, f32[2,4]{1,0:T(2,128)}, u32[]{:S(2)}) copy-start(f32[2,4]{1,0:T(2,128)} %get-tuple-element.9) | copy-start | bytes 100

commit v3 on v2

--- a/solution.py
+++ b/solution.py
@@ -19,13 +19,15 @@
 BF16 = jnp.bfloat16
 MESH = pl.DeviceIdType.MESH
 N_SEM = 256
+SHIFTED = 1024
 PLAN = (
-    "yd0", "q", "yq1", "yq7", "Q", "yq0", "q", "yq2", "D", "Q", "q", "yd0", "yq1", "yq7", "yq0", "yq6", "yq2", "Q",
-    "q", "yd0", "yq3", "yq1", "yq5", "D", "yq7", "yq4", "Q", "d", "yq6", "yq2", "yq3", "yq5", "yq4", "Q", "D",
-    "yq6", "yq3", "d", "yd1", "yd7", "yq5", "Q", "yq4", "oq", "yd1", "D", "Q", "yd7", "d", "yd2", "yd6", "oq",
-    "yd1", "o0", "Q", "D", "yd7", "Q", "o0", "d", "yd3", "yd5", "yd2", "Q", "oq", "Q", "yd6", "d", "yd4", "D", "o0",
-    "yd3", "oq", "P", "yd5", "yd2", "o0", "D", "yd6", "o3", "yd4", "yd3", "o1", "o3", "yd5", "D", "yd4", "o2", "o1",
-    "o2", "o3", "D", "o1", "D", "o2", "o3", "D", "R", "o1", "o2",
+    "yd0", "yq0", "q", "yq1", "yq7", "Q", "x", "D", "yd0", "F", "F", "F", "F", "q", "yq0", "yq2", "F", "F", "yq1",
+    "Q", "F", "F", "x", "yq7", "F", "D", "yd0", "yq6", "q", "yq2", "x", "yq1", "yq3", "Q", "yq7", "yq5", "yq6", "d",
+    "yq2", "D", "q", "yq4", "yq3", "x", "yq5", "yq6", "yq4", "Q", "d", "yd1", "yq3", "yd7", "yq5", "yq4", "oq", "Q",
+    "D", "yd1", "x", "oq", "yd7", "d", "yd2", "yd6", "Q", "x", "D", "yd1", "d", "yd7", "yd3", "yd2", "oq", "Q", "x",
+    "o0", "d", "yd6", "D", "Q", "o0", "yd5", "oq", "yd3", "yd2", "yd4", "E", "yd6", "o3", "D", "yd5", "o0", "yd3",
+    "o1", "o3", "yd4", "E", "Q", "yd5", "D", "o0", "o1", "yd4", "o2", "E", "o3", "Q", "D", "o2", "o1", "E", "Q",
+    "P", "P", "P", "P", "P", "o3", "D", "P", "P", "E", "P", "P", "o2", "D", "R", "R", "R", "S", "o1", "S", "S", "o2",
 )
 
 
@@ -70,7 +72,7 @@
         return dev(z, y, lax.div(mm, X), lax.rem(mm, X))
 
     barrier = pltpu.get_barrier_semaphore()
-    friends = [to_m(k) for k in range(1, G)] + [to_y(k) for k in range(1, Y)] + [to_z(k) for k in range(1, Z)]
+    friends = [to_m(k) for k in range(1, G)] + [to_y(1), to_y(-1), to_z(1), to_z(-1)]
     for friend in friends:
         pl.semaphore_signal(barrier, inc=1, device_id=friend, device_id_type=MESH)
 
@@ -168,9 +170,27 @@
 
     rows_d = 2 * doc_grad.shape[0]
 
+    shifted = min(SHIFTED, quarter)
+    main = half - shifted
+
+    def span(first, size, b):
+        return pl.ds(first, size) if b is None else pl.ds(first + b * (size // 2), size // 2)
+
+    def gd_rows(oz, yy):
+        return pl.ds(pl.multiple_of((oz % Z) * Y * rows_d + yy * rows_d, rows_d), rows_d)
+
     def gd_blk(oz, yy, b=None):
-        at = pl.ds(pl.multiple_of((oz % Z) * Y * rows_d + yy * rows_d, rows_d), rows_d)
-        return gd.at[at, :] if b is None else gd.at[at, pl.ds(b * quarter, quarter)]
+        return gd.at[gd_rows(oz, yy), span(0, main, b)]
+
+    def shift_task():
+        def along(o, b):
+            return gd.at[gd_rows(0, wrap(y + o, Y)), span(main, shifted, b)]
+
+        def group(oz, b):
+            return gd.at[pl.ds((oz % Z) * Y * rows_d, Y * rows_d), span(main, shifted, b)]
+
+        yield from ring_ag(Y, along, lambda o, step, b: along(o, b), to_y)
+        yield from ring_ag(Z, group, lambda o, step, b: group(o - step, b), to_z)
 
     def gq_blk(oz, yy, b=None):
         at = wrap(z + oz, Z) * Y + yy
@@ -209,7 +229,7 @@
         copy.wait_recv()
     pin_q[...] = jnp.dot(inq[...], inb[...], preferred_element_type=F32)
 
-    def in_task(pin, zs, zr, yr, rot, rows, place):
+    def in_task(pin, zs, zr, yr, rot, rows, place, rest):
         def put(v):
             for k in range(Y):
                 yr[Y + k] = v[:, k * wy : (k + 1) * wy]
@@ -230,22 +250,34 @@
         for copy in copies:
             copy.wait_recv()
 
-        def at(o, b):
-            return rot.at[place(o), ds(c, wc) if b is None else ds(c * 2 + b, wc // 2)]
-
-        def there(o, step, b):
-            return rot.at[place(o, step), ds(c, wc) if b is None else ds(c * 2 + b, wc // 2)]
-
-        yield from ring_ag(Z, at, there, to_z)
-        whole = rot.at[:, ds(c, wc)]
-        copy = send(whole, whole, partner)
+        for name in rest:
+            next(tasks[name])
+        yield from spread(rot, place, 0, len(rest) + 1)
+
+    def spread(rot, place, i, parts):
+        size = wc // parts
+
+        def cols_of(b):
+            first, width = (c * parts + i, size) if b is None else ((c * parts + i) * 2 + b, size // 2)
+            return ds(first, width)
+
+        yield from ring_ag(
+            Z, lambda o, b: rot.at[place(o), cols_of(b)], lambda o, step, b: rot.at[place(o, step), cols_of(b)], to_z
+        )
+        part = rot.at[:, cols_of(None)]
+        copy = send(part, part, partner)
         yield
         copy.wait_recv()
 
-    in_q = in_task(pin_q, zs_q, zr_q, yr_q, rot_q, bq, lambda o, step=0: ds(wrap(z + o, Z), bq))
-    in_d = in_task(
-        pin_d, zs_d, zr_d, yr_d, rot_d, bd, lambda o, step=0: pl.ds(((o - step) % Z) * bd, bd)
-    )
+    def place_q(o, step=0):
+        return ds(wrap(z + o, Z), bq)
+
+    def place_d(o, step=0):
+        return pl.ds(((o - step) % Z) * bd, bd)
+
+    in_q = in_task(pin_q, zs_q, zr_q, yr_q, rot_q, bq, place_q, ())
+    in_d = in_task(pin_d, zs_d, zr_d, yr_d, rot_d, bd, place_d, ("E",))
+    tasks["E"] = spread(rot_d, place_d, 1, 2)
     next(in_q)
     l_ind.wait()
     r_ind.wait_recv()
@@ -259,7 +291,7 @@
         [jnp.where(first, own, oth), jnp.where(first, oth, own)], axis=0
     ).astype(BF16)
     ag_d = ring_ag(Z, lambda o, b: gd_blk(o, y, b), lambda o, step, b: gd_blk(o - step, y, b), to_z)
-    tasks.update(d=ag_d, Q=in_q, D=in_d)
+    tasks.update(d=ag_d, x=shift_task(), Q=in_q, D=in_d)
 
     def matmul(a, b, out, at, tile):
         depth = a.shape[1]
@@ -324,9 +356,9 @@
     def ih_copy(i):
         return pltpu.make_async_copy(ih.at[:, ds(i, tile)], ihvp.at[:, ds(i, tile)], lsem.at[16 + i])
 
-    def precondition(i, _):
+    def precondition(i):
         at = ds(i, tile)
-        factor = math.sqrt(dq) / (eig[:, at] + DAMPING)
+        factor = eig[:, at]
         grad = jnp.dot(mq[...], rot_q[:, at], preferred_element_type=F32)
         total = None
         for q in range(QUERIES):
@@ -336,21 +368,37 @@
             total = block if total is None else total + block
         ih[:, at] = total.astype(BF16)
         ih_copy(i).start()
-        return 0
+
+    def factors():
+        yield
+        l_eig.wait()
+        for i in range(n_tiles):
+            if i:
+                yield
+            at = ds(i, tile)
+            eig[:, at] = math.sqrt(dq) / (eig[:, at] + DAMPING)
 
     def precondition_all():
+        yield
         ids_q = query_ids[...]
         for q in range(QUERIES):
             mq[q * cols : (q + 1) * cols, :] = jnp.where(ids_q == q, out_rot[:, 0:dq].astype(F32), 0.0).astype(BF16)
-        l_eig.wait()
-        lax.fori_loop(0, n_tiles, precondition, 0)
-        yield
-
-    def project():
-        matmul(prec, rot_d, proj, slice(0, dd), 512)
-        yield
-
-    tasks.update(P=precondition_all(), R=project())
+        for i in range(n_tiles):
+            if i:
+                yield
+            precondition(i)
+
+    def project(i):
+        size = wc // 2
+        for core in range(CORES):
+            yield
+            at = slice(core * wc + i * size, core * wc + (i + 1) * size)
+            block = lax.dot_general(
+                prec[:, at], rot_d[:, at], (((1,), (1,)), ((), ())), preferred_element_type=F32
+            )
+            proj[...] = block if i + core == 0 else proj[...] + block
+
+    tasks.update(F=factors(), P=precondition_all(), R=project(0), S=project(1))
     for name in PLAN:
         next(tasks[name], None)
     for task in tasks.values():

time: 105 us -> 98.9 us (0.942)
  Pallas kernels: 101 us -> 94.6 us
    pallas_call x1, Pallas kernels: 101 us -> 94.6 us  [shards(): pl.pallas_call(functools.partial(kernel, Z, X, scale), out_shape=(jax.Sha...]
where the time goes in v3:
time: 98.9 us; the launch traced here: 98.8 us
  Pallas kernels  94.6 us (96%)
  local copies, waits for them, and re-layouts  3.51 us (4%)
    pallas_call x1, Pallas kernels, shards(): pl.pallas_call(functools.partial(kernel, Z, X, scale), out_shape=(jax.Sha...  94.6 us
    unnamed x4, local copies, waits for them, and re-layouts  3.51 us

profile of v3, /device:TPU:1, one launch (start us, length us, event | category | flops | bytes accessed | tf_op | source)
XLA Modules:
  0.0 98.8 jit_solution(9576170176623748472)
XLA Ops:
  0.6 94.6 %shard_map.104 = (bf16[448,2048]{1,0:T(8,128)(2,1)}, f32[2,4]{1,0:T(2,128)}) custom-call(bf16[512,128]{1,0:T(8,128)(2,1)} %doc_in.1, bf16[256,128]{1,0:T(8,128)(2,1)} %query_in.1, bf16[8,7168]{1,0:T(8,128)(2,1)} %doc_grad.1, bf16[4,7168]{1,0:T(4,128)(2,1)} %query_grad.1, s32[1,512]{1,0:T(1,128)} %bitcast.8, s32[1,256]{1,0:T(1,128)} %bitcast.9, ...), custom_call_target="tpu_custom_call" | custom-call | tf_op jit(solution)/shard_map/pallas_call | solution.py:459
  95.2 0.0 copy-start
  95.3 2.9 %copy.13 = bf16[2048,448]{0,1:T(8,128)(2,1)} copy(bf16[2048,448]{0,1:T(8,128)(2,1)} %bitcast.7) | data formatting | bytes 3670016
  98.2 0.0 copy-done
  98.2 0.6 copy.14
Async XLA Ops:
  95.2 3.0 %copy-start = (f32[2,4]{1,0:T(2,128)S(1)}, f32[2,4]{1,0:T(2,128)}, u32[]{:S(2)}) copy-start(f32[2,4]{1,0:T(2,128)} %get-tuple-element.9) | copy-start | bytes 100

commit v4 on v3

--- a/solution.py
+++ b/solution.py
@@ -41,7 +41,7 @@
     ihvp, scores,
     inq, ind, inb, gd_own, gd_oth, gq_own, gq_oth, gq_f, gd, gq, gq2, bb, eig,
     pin_q, pin_d, zs_q, zr_q, zs_d, zr_d, yr_q, yr_d, rot_q, rot_d,
-    part, p_rcv, x_snd, x_rcv, out_rot, mq, prec, ih, proj, sc_a, sc_b, sc_c,
+    part, p_rcv, x_snd, x_rcv, out_rot, mq, prec, proj, sc_a, sc_b, sc_c,
     ssem, rsem, lsem,
 ):
     tok, x = lax.axis_index("tok"), lax.axis_index("feat")
@@ -72,7 +72,8 @@
         return dev(z, y, lax.div(mm, X), lax.rem(mm, X))
 
     barrier = pltpu.get_barrier_semaphore()
-    friends = [to_m(k) for k in range(1, G)] + [to_y(1), to_y(-1), to_z(1), to_z(-1)]
+    friends = [partner] + [dev(z, y, c, wrap(x + k, X)) for k in range(1, X)]
+    friends += [to_y(1), to_y(-1), to_z(1), to_z(-1)]
     for friend in friends:
         pl.semaphore_signal(barrier, inc=1, device_id=friend, device_id_type=MESH)
 
@@ -353,9 +354,6 @@
     tile = 256
     n_tiles = eig.shape[1] // tile
 
-    def ih_copy(i):
-        return pltpu.make_async_copy(ih.at[:, ds(i, tile)], ihvp.at[:, ds(i, tile)], lsem.at[16 + i])
-
     def precondition(i):
         at = ds(i, tile)
         factor = eig[:, at]
@@ -366,8 +364,7 @@
             prec[q * cols : (q + 1) * cols, at] = block
             block = block.astype(F32)
             total = block if total is None else total + block
-        ih[:, at] = total.astype(BF16)
-        ih_copy(i).start()
+        ihvp[:, at] = total.astype(BF16)
 
     def factors():
         yield
@@ -430,11 +427,6 @@
     value = exchange(sc_c, z, Z, to_z, value)
     scores[...] = value[0:QUERIES, 0:DOCS] * scale
 
-    def ih_wait(i, _):
-        ih_copy(i).wait()
-        return 0
-
-    lax.fori_loop(0, n_tiles, ih_wait, 0)
     for copy in sent:
         copy.wait_send()
 
@@ -459,11 +451,11 @@
     ihvp, scores = pl.pallas_call(
         functools.partial(kernel, Z, X, scale),
         out_shape=(
-            jax.ShapeDtypeStruct((cols, width), BF16),
+            pltpu.VMEM((cols, width), BF16),
             jax.ShapeDtypeStruct((QUERIES, DOCS), F32),
         ),
         in_specs=[any_, any_, any_, any_, in_vmem, in_vmem, any_, any_, any_],
-        out_specs=(any_, in_vmem),
+        out_specs=(in_vmem, in_vmem),
         scratch_shapes=[
             vmem((dq, CORES * nf), BF16), vmem((dd, CORES * nf), BF16), vmem((CORES * nf, wc), BF16),
             vmem((n_docs, half), BF16), vmem((n_docs, half), BF16),
@@ -477,7 +469,7 @@
             vmem((dq, width), BF16), vmem((dd, width), BF16),
             vmem((2 * cols, dq + dd), F32), vmem((cols, dq + dd), F32),
             vmem((cols, dq + dd), X_DT), vmem((X, cols // X, dq + dd), X_DT), vmem((cols, dq + dd), BF16),
-            vmem((QUERIES * cols, dq), BF16), vmem((QUERIES * cols, width), BF16), vmem((cols, width), BF16),
+            vmem((QUERIES * cols, dq), BF16), vmem((QUERIES * cols, width), BF16),
             vmem((QUERIES * cols, dd), F32),
             vmem((CORES * X, 8, 128), F32), vmem((Y, 8, 128), F32), vmem((Z, 8, 128), F32),
             pltpu.SemaphoreType.DMA((N_SEM,)), pltpu.SemaphoreType.DMA((N_SEM,)), pltpu.SemaphoreType.DMA((32,)),

time: 98.9 us -> 97.1 us (0.982)
  local copies, waits for them, and re-layouts: 3.51 us -> 1.8 us
    unnamed x4, local copies, waits for them, and re-layouts: 3.51 us -> 1.8 us
where the time goes in v4:
time: 97.1 us; the launch traced here: 96.7 us
  Pallas kernels  94.3 us (97%)
  local copies, waits for them, and re-layouts  1.8 us (2%)
    pallas_call x1, Pallas kernels, shards(): pl.pallas_call(functools.partial(kernel, Z, X, scale), out_shape=(pltpu.V...  94.3 us

profile of v4, /device:TPU:1, one launch (start us, length us, event | category | flops | bytes accessed | tf_op | source)
XLA Modules:
  0.0 96.7 jit_solution(3915711982599910788)
XLA Ops:
  0.6 94.3 %shard_map.104 = (bf16[448,2048]{1,0:T(8,128)(2,1)S(1)}, f32[2,4]{1,0:T(2,128)}) custom-call(bf16[512,128]{1,0:T(8,128)(2,1)} %doc_in.1, bf16[256,128]{1,0:T(8,128)(2,1)} %query_in.1, bf16[8,7168]{1,0:T(8,128)(2,1)} %doc_grad.1, bf16[4,7168]{1,0:T(4,128)(2,1)} %query_grad.1, s32[1,512]{1,0:T(1,128)} %bitcast.8, s32[1,256]{1,0:T(1,128)} %bitcast.9, ...), custom_call_target="tpu_custom_call" | custom-call | tf_op jit(solution)/shard_map/pallas_call | solution.py:451
  94.9 0.0 copy-start
  94.9 1.2 %copy.13 = bf16[2048,448]{0,1:T(8,128)(2,1)} copy(bf16[2048,448]{0,1:T(8,128)(2,1)S(1)} %bitcast.5) | data formatting | bytes 3670016
  96.1 0.0 copy-done
  96.1 0.6 copy.14
Async XLA Ops:
  94.9 1.2 %copy-start = (f32[2,4]{1,0:T(2,128)S(1)}, f32[2,4]{1,0:T(2,128)}, u32[]{:S(2)}) copy-start(f32[2,4]{1,0:T(2,128)} %get-tuple-element.11) | copy-start | bytes 100

commit v5 on v4

--- a/solution.py
+++ b/solution.py
@@ -14,11 +14,12 @@
 Y = 4
 CORES = 2
 RS_DT = jnp.bfloat16
-X_DT = jnp.float32
+X_DT = jnp.bfloat16
 F32 = jnp.float32
 BF16 = jnp.bfloat16
 MESH = pl.DeviceIdType.MESH
 N_SEM = 256
+IN_FLIGHT = 48
 SHIFTED = 1024
 PLAN = (
     "yd0", "yq0", "q", "yq1", "yq7", "Q", "x", "D", "yd0", "F", "F", "F", "F", "q", "yq0", "yq2", "F", "F", "yq1",
@@ -41,7 +42,7 @@
     ihvp, scores,
     inq, ind, inb, gd_own, gd_oth, gq_own, gq_oth, gq_f, gd, gq, gq2, bb, eig,
     pin_q, pin_d, zs_q, zr_q, zs_d, zr_d, yr_q, yr_d, rot_q, rot_d,
-    part, p_rcv, x_snd, x_rcv, out_rot, mq, prec, proj, sc_a, sc_b, sc_c,
+    part, p_rcv, xs_q, xr_q, xs_d, xr_d, out_rot, mq, prec, proj, sc_a, sc_b, sc_c,
     ssem, rsem, lsem,
 ):
     tok, x = lax.axis_index("tok"), lax.axis_index("feat")
@@ -113,6 +114,14 @@
         copy.start()
         sent.append(copy)
         return copy
+
+    settled = []
+
+    def settle(few):
+        while len(settled) < len(sent) - few:
+            copy = sent[len(settled)]
+            copy.wait_send()
+            settled.append(copy)
 
     r_gq = send(query_grad.at[:, ds(oc, half)], gq_oth, partner)
     r_inq = send(query_in, inq.at[:, ds(c, nf)], partner)
@@ -308,24 +317,25 @@
 
     share = cols // X
 
-    def out_task(grads, at):
+    def out_task(grads, at, snd, rcv, own):
         matmul(bb, grads, part, at, 896)
         swap = send(part.at[0:cols, at], p_rcv.at[:, at], partner)
         yield
         swap.wait_recv()
-        x_snd[:, at] = (part[cols : 2 * cols, at] + p_rcv[:, at]).astype(X_DT)
+        total = part[cols : 2 * cols, at] + p_rcv[:, at]
+        p_rcv[:, at] = total
+        snd[:, own] = total.astype(snd.dtype)
         copies = []
         for k in range(1, X):
             to = wrap(x + k, X)
-            copies.append(send(x_snd.at[ds(to, share), at], x_rcv.at[x, :, at], dev(z, y, c, to)))
+            copies.append(send(snd.at[ds(to, share), own], rcv.at[x, :, own], dev(z, y, c, to)))
         yield
         for copy in copies:
             copy.wait_recv()
         mine = ds(x, share)
-        x_rcv[x, :, at] = x_snd[mine, at]
-        total = x_rcv[0, :, at].astype(F32)
+        total = p_rcv[mine, at]
         for k in range(1, X):
-            total = total + x_rcv[k, :, at].astype(F32)
+            total = total + rcv[wrap(x + k, X), :, own].astype(F32)
         out_rot[mine, at] = total.astype(BF16)
         copies = []
         for k in range(1, X):
@@ -342,14 +352,13 @@
             gq2[:, h * quarter : (h + 1) * quarter] = (
                 gq[:, h * rows : (h + 1) * rows, :].astype(F32).reshape(dq, quarter).astype(BF16)
             )
-        yield from out_task(gq2, slice(0, dq))
+        yield from out_task(gq2, slice(0, dq), xs_q, xr_q, slice(0, dq))
 
     chunk = 2 * (dd // Z)
     tasks["oq"] = out_queries()
     for i in range(Z // 2):
-        tasks["o%d" % i] = out_task(
-            gd.at[i * chunk : (i + 1) * chunk, :], slice(dq + i * chunk, dq + (i + 1) * chunk)
-        )
+        own = slice(i * chunk, (i + 1) * chunk)
+        tasks["o%d" % i] = out_task(gd.at[own, :], slice(dq + own.start, dq + own.stop), xs_d, xr_d, own)
 
     tile = 256
     n_tiles = eig.shape[1] // tile
@@ -398,6 +407,7 @@
     tasks.update(F=factors(), P=precondition_all(), R=project(0), S=project(1))
     for name in PLAN:
         next(tasks[name], None)
+        settle(IN_FLIGHT)
     for task in tasks.values():
         for _ in task:
             pass
@@ -418,6 +428,7 @@
     def exchange(buf, me, n, to, value):
         buf[me] = value
         copies = [send(buf.at[me], buf.at[me], to(k)) for k in range(1, n)]
+        settle(n - 1)
         for copy in copies:
             copy.wait_recv()
         return jnp.sum(buf[...], axis=0)
@@ -427,8 +438,7 @@
     value = exchange(sc_c, z, Z, to_z, value)
     scores[...] = value[0:QUERIES, 0:DOCS] * scale
 
-    for copy in sent:
-        copy.wait_send()
+    settle(0)
 
 
 def shards(
@@ -468,7 +478,8 @@
             vmem((2 * Y, bq, wy), F32), vmem((2 * Y, bd, wy), F32),
             vmem((dq, width), BF16), vmem((dd, width), BF16),
             vmem((2 * cols, dq + dd), F32), vmem((cols, dq + dd), F32),
-            vmem((cols, dq + dd), X_DT), vmem((X, cols // X, dq + dd), X_DT), vmem((cols, dq + dd), BF16),
+            vmem((cols, dq), F32), vmem((X, cols // X, dq), F32), vmem((cols, dd), X_DT), vmem((X, cols // X, dd), X_DT),
+            vmem((cols, dq + dd), BF16),
             vmem((QUERIES * cols, dq), BF16), vmem((QUERIES * cols, width), BF16),
             vmem((QUERIES * cols, dd), F32),
             vmem((CORES * X, 8, 128), F32), vmem((Y, 8, 128), F32), vmem((Z, 8, 128), F32),

time: 97.1 us -> 95.6 us (0.985)
  Pallas kernels: 94.3 us -> 92.7 us
    pallas_call x1, Pallas kernels: 94.3 us -> 92.7 us  [shards(): pl.pallas_call(functools.partial(kernel, Z, X, scale), out_shape=(pltpu.V...]
where the time goes in v5:
time: 95.6 us; the launch traced here: 95.2 us
  Pallas kernels  92.7 us (97%)
  local copies, waits for them, and re-layouts  1.8 us (2%)
    pallas_call x1, Pallas kernels, shards(): pl.pallas_call(functools.partial(kernel, Z, X, scale), out_shape=(pltpu.V...  92.7 us

profile of v5, /device:TPU:1, one launch (start us, length us, event | category | flops | bytes accessed | tf_op | source)
XLA Modules:
  0.0 95.2 jit_solution(3170079831045901938)
XLA Ops:
  0.6 92.7 %shard_map.104 = (bf16[448,2048]{1,0:T(8,128)(2,1)S(1)}, f32[2,4]{1,0:T(2,128)}) custom-call(bf16[512,128]{1,0:T(8,128)(2,1)} %doc_in.1, bf16[256,128]{1,0:T(8,128)(2,1)} %query_in.1, bf16[8,7168]{1,0:T(8,128)(2,1)} %doc_grad.1, bf16[4,7168]{1,0:T(4,128)(2,1)} %query_grad.1, s32[1,512]{1,0:T(1,128)} %bitcast.8, s32[1,256]{1,0:T(1,128)} %bitcast.9, ...), custom_call_target="tpu_custom_call" | custom-call | tf_op jit(solution)/shard_map/pallas_call | solution.py:461
  93.4 0.0 copy-start
  93.4 1.2 %copy.13 = bf16[2048,448]{0,1:T(8,128)(2,1)} copy(bf16[2048,448]{0,1:T(8,128)(2,1)S(1)} %bitcast.5) | data formatting | bytes 3670016
  94.6 0.0 copy-done
  94.6 0.6 copy.14
Async XLA Ops:
  93.4 1.2 %copy-start = (f32[2,4]{1,0:T(2,128)S(1)}, f32[2,4]{1,0:T(2,128)}, u32[]{:S(2)}) copy-start(f32[2,4]{1,0:T(2,128)} %get-tuple-element.11) | copy-start | bytes 100
